TPU v7x, 32 devices: a whole 2x2x4 slice. The times are simulated.
32 devices in a mesh: groups: 2 (over y), tiles: 4 (over z), band: 2 (over x), stokes: 2 (over core).
Axes of the slice: x: 2, y: 2, z: 4, core: 2. Of those that a mesh axis runs over, the one named last changes fastest.
Arguments:
- right_side: float32 [3, 128, 2048], P(None, ('groups', 'tiles'), ('band', 'stokes')), parts along dimension 1, may hold values from -4 to 4
- noise_block: float32 [6, 128, 2048], P(None, ('groups', 'tiles'), ('band', 'stokes')), parts along dimension 1, may hold values from -0.09 to 0.4, as said below
- edges: float32 [2, 128, 2048], P(None, ('groups', 'tiles'), ('band', 'stokes')), parts along dimension 1, may hold values from 0.5 to 2
Outputs:
- correction: float32 [3, 128, 2048], P(None, ('groups', 'tiles'), ('band', 'stokes')), parts along dimension 1
There are 2 independent parts, one for each index of `groups`. A program takes and returns all parts, laid end to end along the dimension named above; each array names one. Nothing has to cross between parts.
Inputs may be any that keep to these rules, and one draw needn't show every extreme that they name: `noise_block`: entries 0 to 2 are positive and each exceeds the sum of the magnitudes of the two couplings in its row of the 3 x 3 matrix.
All inputs are finite; a program needn't handle non-finite values.
Results may differ from a plain program's by a relative error of at most 0.00002.
Values sent between devices are 32-bit elements; how exact they have to be, the bound alone decides.
A program may use at most 64 MiB of HBM per device.

v0:
```python
import functools
import itertools

import jax
import jax.numpy as jnp
from jax import lax
from jax.experimental import pallas as pl
from jax.experimental.pallas import tpu as pltpu
from jax.sharding import PartitionSpec as P

OMEGA = 0.8
COARSE_SWEEPS = 8
HALO = 8
SIDE = 128
DEEP = 11
BUFFERS = 12
NEAR_ROWS = (6, 6, 6, 6, 6, 6, 5, 5, 5, 7, 6)
MESH = pl.DeviceIdType.MESH
F32 = jnp.float32


def rounded(x):
    return x.astype(jnp.bfloat16).astype(F32)


def dot(x, y):
    n = x.shape[0]
    high = rounded(x)
    rest = x - high
    mid = rounded(rest)
    pieces = jnp.concatenate([high, mid, rest - mid], 0)
    z = jnp.dot(pieces, y, precision=lax.Precision.DEFAULT, preferred_element_type=F32)
    return z[:n] + (z[n : 2 * n] + z[2 * n :])


def iota(shape, dim):
    return lax.broadcasted_iota(jnp.int32, shape, dim)


def ones(hit):
    return jnp.where(hit, 1.0, 0.0).astype(F32)


def half(i):
    return lax.shift_right_logical(i, 1)


def pool_matrix(n, m, odd=False):
    c, j = iota((n, m), 0), iota((n, m), 1)
    hit = c == 2 * j + 1
    return ones(hit if odd else hit | (c == 2 * j))


def spread_matrix(n, m):
    c, j = iota((n, m), 0), iota((n, m), 1)
    return ones(c == half(j))


def ring_pool(cut, odd=False):
    c, j = iota((SIDE, SIDE), 0), iota((SIDE, SIDE), 1)
    hit = j == half(c) + jnp.where(c >= cut, 64, 0)
    return ones(hit & ((c & 1) == 1) if odd else hit)


def ring_spread(n, m, cut):
    c, j = iota((n, m), 0), iota((n, m), 1)
    return ones(c == half(j) + jnp.where(j >= cut, 64, 0))


def chunks(a):
    return range(a.shape[1] // 8)


def setup(a, aux):
    for q in chunks(a):
        rows = slice(8 * q, 8 * q + 8)
        down, right = a[9, rows], a[10, rows]
        if q == 0:
            up = jnp.where(iota(down.shape, 0) == 0, 0.0, pltpu.roll(down, 1, 0))
        else:
            up = a[9, 8 * q - 1 : 8 * q + 7]
        left = pltpu.roll(right, 1, 1)
        total = down + up + right + left
        aux[0, rows], aux[1, rows], aux[2, rows] = up, left, total
        for k in range(3):
            aux[3 + k, rows] = jnp.where(down > 0, OMEGA / (a[3 + k, rows] + total), 0.0)


def first(a, aux, v):
    for q in chunks(a):
        rows = slice(8 * q, 8 * q + 8)
        for k in range(3):
            v[k, 8 + 8 * q : 16 + 8 * q] = aux[3 + k, rows] * a[k, rows]


def residual_at(a, aux, v, q):
    rows = slice(8 * q, 8 * q + 8)
    mid = [v[k, 8 + 8 * q : 16 + 8 * q] for k in range(3)]
    n = [a[3 + i, rows] for i in range(6)]
    down, right, up, left, total = a[9, rows], a[10, rows], aux[0, rows], aux[1, rows], aux[2, rows]
    width = mid[0].shape[1]
    image = [
        n[0] * mid[0] + n[3] * mid[1] + n[4] * mid[2],
        n[3] * mid[0] + n[1] * mid[1] + n[5] * mid[2],
        n[4] * mid[0] + n[5] * mid[1] + n[2] * mid[2],
    ]
    out = []
    for k in range(3):
        near = (
            down * v[k, 9 + 8 * q : 17 + 8 * q]
            + up * v[k, 7 + 8 * q : 15 + 8 * q]
            + right * pltpu.roll(mid[k], width - 1, 1)
            + left * pltpu.roll(mid[k], 1, 1)
        )
        out.append(a[k, rows] - (image[k] + total * mid[k] - near))
    return mid, out


def sweep(a, aux, src, dst, which=None):
    for q in chunks(a) if which is None else which:
        mid, res = residual_at(a, aux, src, q)
        for k in range(3):
            dst[k, 8 + 8 * q : 16 + 8 * q] = mid[k] + aux[3 + k, 8 * q : 8 * q + 8] * res[k]


def residual(a, aux, v, r):
    height = a.shape[1]
    for q in chunks(a):
        _, res = residual_at(a, aux, v, q)
        for k in range(3):
            r[k * height + 8 * q : k * height + 8 * q + 8, :] = res[k]


def pool_lanes(x, matrix, tail=None):
    n = matrix.shape[0]
    width = x.shape[1]
    parts = []
    for b in range(0, width, n):
        if b + n <= width:
            parts.append(dot(x[:, b : b + n], matrix))
        else:
            parts.append(dot(x[:, b:width], matrix[: width - b] if tail is None else tail))
    return parts


def pool_rows(parts, st, odd=False):
    st = st()
    out = []
    for b, part in enumerate(parts):
        n = part.shape[0]
        st[b, 0:n, :] = part
        top = st[b, pl.ds(1, n // 2, stride=2), :]
        out.append(top if odd else top + st[b, pl.ds(0, n // 2, stride=2), :])
    return out


def coarsen_coefficients(arrays, st, even, odd):
    h = arrays[0].shape[0]
    parts = pool_lanes(jnp.concatenate(arrays[:7], 0), even)
    noise = pool_rows([p[: 6 * h] for p in parts], st)
    down = pool_rows([p[6 * h :] for p in parts], st, odd=True)
    right = pool_rows(pool_lanes(arrays[7], odd), st)
    h = h // 2
    out = []
    for i in range(6):
        out.append([p[i * h : i * h + h] for p in noise])
    return out + [down, right]


def spread_rows(parts, st):
    st = st()
    for b, part in enumerate(parts):
        n = part.shape[0]
        st[b, pl.ds(0, n, stride=2), :] = part
        st[b, pl.ds(1, n, stride=2), :] = part
    return st


def put(a, channel, row, parts, tile=0):
    for b, part in enumerate(parts, tile):
        a[channel, row : row + part.shape[0], SIDE * b : SIDE * b + SIDE] = part


def add_spread(v, dst, st, stride, blocks, height, row0=0):
    for k in range(3):
        for b in range(blocks):
            lanes = slice(SIDE * b, SIDE * b + SIDE)
            dst[k, 8 : 8 + height, lanes] = v[k, 8 : 8 + height, lanes] + st[b, stride * k + row0 : stride * k + row0 + height, :]


def kernel(
    T, NB, NS, stack, out,
    a0, x0, u0, w0, r0, a1, x1, u1, w1, r1, a2, x2, u2, w2, r2, a3, x3, u3, w3, r3, a4, x4, u4, w4,
    tiles, win, sent, got, rows_sent, rows_got,
    coef_own, coef_side, coef_pack, src_own, src_side, src_pack, side_rows,
    in_sem, halo_send, halo_recv, coef_send, coef_recv, src_send, src_recv, row_send, row_recv,
):
    turn = itertools.cycle(range(BUFFERS))

    def st():
        return tiles.at[next(turn)]

    t = lax.axis_index("tiles")
    col = lax.axis_index("band") * NS + lax.axis_index("stokes")
    cols = NB * NS
    h, w = stack.shape[1], stack.shape[2]
    has = {-1: col > 0, 0: None, 1: col < cols - 1}
    rowhas = {-1: t > 0, 0: None, 1: t < T - 1}

    def when(*conds):
        conds = [c for c in conds if c is not None]
        if not conds:
            return lambda f: f()
        return pl.when(functools.reduce(jnp.logical_and, conds))

    def device(tile, dc):
        c = col + dc
        return {"tiles": tile, "band": c // NS, "stokes": lax.rem(c, NS)}

    own_rows, own_cols = slice(HALO, HALO + h), slice(0, w)
    load = pltpu.make_async_copy(stack, a0.at[:, own_rows, own_cols], in_sem.at[0])
    load.start()

    partners = [(dt, dc) for dc in (-1, 0, 1) for dt in range(T) if dt or dc]
    barrier = pltpu.get_barrier_semaphore()
    for dt, dc in partners:
        @when(has[dc])
        def _(dt=dt, dc=dc):
            pl.semaphore_signal(barrier, inc=1, device_id=device(lax.rem(t + dt, T), dc), device_id_type=MESH)

    @pl.when(t == 0)
    def _():
        got[:, 0:HALO] = jnp.zeros_like(got[:, 0:HALO])
        side_rows[0] = jnp.zeros_like(side_rows[0])

    @pl.when(t == T - 1)
    def _():
        got[:, HALO + h :] = jnp.zeros_like(got[:, HALO + h :])
        side_rows[1] = jnp.zeros_like(side_rows[1])

    @pl.when(col == 0)
    def _():
        got[0] = jnp.zeros_like(got[0])
        coef_side[:, 0] = jnp.zeros_like(coef_side[:, 0])
        src_side[:, 0] = jnp.zeros_like(src_side[:, 0])

    @pl.when(col == cols - 1)
    def _():
        got[1] = jnp.zeros_like(got[1])
        coef_side[:, 1] = jnp.zeros_like(coef_side[:, 1])
        src_side[:, 1] = jnp.zeros_like(src_side[:, 1])

    a0[:, 0:HALO, own_cols] = jnp.zeros_like(a0[:, 0:HALO, own_cols])
    a0[:, HALO + h :, own_cols] = jnp.zeros_like(a0[:, HALO + h :, own_cols])
    for a in (a1, a3, a4):
        a[...] = jnp.zeros_like(a)
    for v in (x0, u0, x1, u1, x2, u2, x3, u3, x4, u4):
        v[:, 0:8, :] = jnp.zeros_like(v[:, 0:8, :])
        n = v.shape[1]
        v[:, n - 8 : n, :] = jnp.zeros_like(v[:, n - 8 : n, :])

    load.wait()

    lane = iota((8, SIDE), 1)
    for q in range(h // 8):
        rows = slice(HALO + 8 * q, HALO + 8 * q + 8)
        head = tail = jnp.zeros((8, SIDE), F32)
        for i in range(11):
            here = (lane >= DEEP * i) & (lane < DEEP * i + DEEP)
            one, two = a0[i, rows, 0:SIDE], a0[i, rows, w - SIDE : w]
            head = jnp.where(here, pltpu.roll(one, DEEP * i, 1) if i else one, head)
            tail = jnp.where(here, pltpu.roll(two, (DEEP * i + DEEP) % SIDE, 1), tail)
        sent[0, 8 * q : 8 * q + 8], sent[1, 8 * q : 8 * q + 8] = head, tail
    at = 0
    for i, n in enumerate(NEAR_ROWS):
        rows_sent[0, at : at + n] = a0[i, HALO : HALO + n, own_cols]
        rows_sent[1, at : at + n] = a0[i, HALO + h - n : HALO + h, own_cols]
        at += n

    sides = 1 + jnp.where(col > 0, 1, 0) + jnp.where(col < cols - 1, 1, 0)
    pl.semaphore_wait(barrier, sides * T - 1)

    row_dst = {-1: slice(HALO + h, 2 * HALO + h), 0: own_rows, 1: slice(0, HALO)}
    part_src = {-1: slice(0, HALO), 0: slice(0, h), 1: slice(h - HALO, h)}

    def halo(dr, dc):
        i = (dr + 1) * 3 + dc + 1
        if dc:
            src = sent.at[(dc + 1) // 2, part_src[dr]]
            dst = got.at[(1 - dc) // 2, row_dst[dr]]
        else:
            src, dst = rows_sent.at[(dr + 1) // 2], rows_got.at[(1 - dr) // 2]
        return pltpu.make_async_remote_copy(
            src_ref=src,
            dst_ref=dst,
            send_sem=halo_send.at[i],
            recv_sem=halo_recv.at[i],
            device_id=device(t + dr, dc),
            device_id_type=MESH,
        )

    ways = [(0, -1), (0, 1), (-1, -1), (-1, 1), (1, -1), (1, 1), (-1, 0), (1, 0)]
    for dr, dc in ways:
        @when(rowhas[dr], has[dc])
        def _(dr=dr, dc=dc):
            halo(dr, dc).start()

    def gather(own, side, pack, send, recv, dt, dc):
        if dc:
            src, dst = pack.at[(dc + 1) // 2], side.at[t, (1 - dc) // 2]
        else:
            src, dst = own.at[t], own.at[t]
        return pltpu.make_async_remote_copy(
            src_ref=src,
            dst_ref=dst,
            send_sem=send.at[dt, dc + 1],
            recv_sem=recv.at[t, 1 - dc],
            device_id=device(lax.rem(t + dt, T), dc),
            device_id_type=MESH,
        )

    def arrival(own, side, pack, send, recv, dt, dc):
        s = lax.rem(t + dt, T)
        dst = side.at[s, (dc + 1) // 2] if dc else own.at[s]
        return pltpu.make_async_remote_copy(
            src_ref=dst,
            dst_ref=dst,
            send_sem=send.at[dt, dc + 1],
            recv_sem=recv.at[s, dc + 1],
            device_id=device(s, dc),
            device_id_type=MESH,
        )

    coef = (coef_own, coef_side, coef_pack, coef_send, coef_recv)
    src = (src_own, src_side, src_pack, src_send, src_recv)

    def scatter(x, way):
        own, pack = way[0], way[2]
        n = x.shape[0] // 2
        low = iota((n, SIDE), 1) < 64
        own[t] = x
        pack[0] = jnp.where(low, x[:n], pltpu.roll(x[n:], 64, 1))
        pack[1] = jnp.where(low, pltpu.roll(x[:n], 64, 1), x[n:])
        for dt, dc in partners:
            @when(has[dc])
            def _(dt=dt, dc=dc):
                gather(*way, dt, dc).start()

    def assemble(way, channel, count):
        for dt, dc in partners:
            @when(has[dc])
            def _(dt=dt, dc=dc):
                arrival(*way, dt, dc).wait_recv()
        own, side = way[:2]
        n = side.shape[2]
        low = iota((n, SIDE), 1) < 64

        def beside(s):
            left, right = side[s, 0], side[s, 1]
            return jnp.concatenate(
                [jnp.where(low, right, pltpu.roll(left, 64, 1)), jnp.where(low, pltpu.roll(right, 64, 1), left)], 0
            )

        for j in range(T // 2):
            for c in range(2):
                one, two = (beside(2 * j), beside(2 * j + 1)) if c else (own[2 * j], own[2 * j + 1])
                for i in range(count):
                    a2[channel + i, 8 * j : 8 * j + 8, SIDE * c : SIDE * c + SIDE] = jnp.concatenate(
                        [one[4 * i : 4 * i + 4], two[4 * i : 4 * i + 4]], 0
                    )

    even, odd = pool_matrix(256, 128), pool_matrix(256, 128, odd=True)
    even_ring, odd_ring = ring_pool(64), ring_pool(64, odd=True)
    wide = spread_matrix(128, 256)

    fine = [a0[3 + i, own_rows, own_cols] for i in range(8)]
    mid = coarsen_coefficients(fine, st, even, odd)
    for i in range(8):
        put(a1, 3 + i, 8, mid[i])
    mid = [jnp.concatenate(parts, 1) for parts in mid]
    low = [parts[0] for parts in coarsen_coefficients(mid, st, even, odd)]
    scatter(jnp.concatenate(low, 0), coef)

    for dr, dc in ways:
        if dc:
            @when(rowhas[dr], has[dc])
            def _(dr=dr, dc=dc):
                halo(-dr, -dc).wait_recv()

    for q in range(a0.shape[1] // 8):
        rows = slice(8 * q, 8 * q + 8)
        for i in range(11):
            right = pltpu.roll(got[1, rows], SIDE - DEEP * i, 1) if i else got[1, rows]
            left = pltpu.roll(got[0, rows], SIDE - DEEP - DEEP * i, 1)
            a0[i, rows, w : w + SIDE] = jnp.where(
                lane < DEEP, right, jnp.where(lane >= SIDE - DEEP, left, 0.0)
            )

    ends = [a0[3 + i, :, w : w + SIDE] for i in range(8)]
    for i, parts in enumerate(coarsen_coefficients(ends, st, even_ring, odd_ring)):
        put(a1, 3 + i, 4, parts, 2)

    for dr in (-1, 1):
        @when(rowhas[dr])
        def _(dr=dr):
            halo(-dr, 0).wait_recv()
            at = 0
            for i, n in enumerate(NEAR_ROWS):
                top = HALO - n if dr < 0 else HALO + h
                a0[i, top : top + n, own_cols] = rows_got[(dr + 1) // 2, at : at + n]
                at += n

    setup(a0, w0)
    first(a0, w0, x0)
    sweep(a0, w0, x0, u0)
    residual(a0, w0, u0, r0)
    source = pool_rows(pool_lanes(r0[...], even, even_ring), st)
    h1 = a0.shape[1] // 2
    for k in range(3):
        put(a1, k, 4, [p[k * h1 : k * h1 + h1] for p in source])
    beside = [
        jnp.concatenate([a0[3 + i, 0:HALO, own_cols], a0[3 + i, HALO + h :, own_cols]], 0) for i in range(8)
    ]
    for i, parts in enumerate(coarsen_coefficients(beside, st, even, odd)):
        put(a1, 3 + i, 4, [p[:4] for p in parts])
        put(a1, 3 + i, 16, [p[4:] for p in parts])
    setup(a1, w1)
    first(a1, w1, x1)
    sweep(a1, w1, x1, u1)
    residual(a1, w1, u1, r1)
    own = dot(r1[:, 0:256], even)
    source = pool_rows([own], st)[0]
    packed = [source[12 * k + 4 : 12 * k + 8] for k in range(3)]
    scatter(jnp.concatenate(packed + [jnp.zeros((4, SIDE), F32)], 0), src)

    def rows_copy(dr):
        i = (dr + 1) // 2
        return pltpu.make_async_remote_copy(
            src_ref=u1.at[:, 16:24, :],
            dst_ref=side_rows.at[1 - i],
            send_sem=row_send.at[i],
            recv_sem=row_recv.at[1 - i],
            device_id=device(t + dr, 0),
            device_id_type=MESH,
        )

    for dr in (-1, 1):
        @when(rowhas[dr])
        def _(dr=dr):
            rows_copy(dr).start()

    assemble(coef, 3, 8)
    setup(a2, w2)
    last, last_odd = ring_pool(96), ring_pool(96, odd=True)
    for a, b, aux, p, p_odd in ((a2, a3, w3, even, odd), (a3, a4, w4, last, last_odd)):
        for i, parts in enumerate(coarsen_coefficients([a[3 + i] for i in range(8)], st, p, p_odd)):
            put(b, 3 + i, 0, parts)
        setup(b, aux)
    assemble(src, 0, 3)

    for a, aux, x, u, r, b, p in ((a2, w2, x2, u2, r2, a3, even), (a3, w3, x3, u3, r3, a4, last)):
        first(a, aux, x)
        sweep(a, aux, x, u)
        residual(a, aux, u, r)
        source = pool_rows(pool_lanes(r[...], p), st)
        n = a.shape[1] // 2
        for k in range(3):
            put(b, k, 0, [z[k * n : k * n + n] for z in source])
    first(a4, w4, x4)
    now, then = x4, u4
    for _ in range(COARSE_SWEEPS - 1):
        sweep(a4, w4, now, then)
        now, then = then, now
    coarse = now
    for a, aux, x, u in ((a3, w3, x3, u3), (a2, w2, x2, u2)):
        n = coarse.shape[1] - 16
        y = jnp.concatenate([coarse[k, 8 : 8 + n] for k in range(3)], 0)
        z = dot(y, wide if a is a2 else ring_spread(SIDE, SIDE, 96))
        parts = [z[:, b : b + SIDE] for b in range(0, z.shape[1], SIDE)]
        add_spread(u, x, spread_rows(parts, st), 2 * n, len(parts), a.shape[1])
        sweep(a, aux, x, u)
        sweep(a, aux, u, x)
        coarse = x

    for s in range(T):
        @pl.when(t == s)
        def _(s=s):
            for k in range(3):
                win[16 * k : 16 * k + 16, :] = x2[k, 4 + 4 * s : 20 + 4 * s]
    y = dot(win[...], ring_spread(256, 384, 320))
    spread = spread_rows([y[:, 128 * b : 128 * b + 128] for b in range(3)], st)
    for dr in (-1, 1):
        @when(rowhas[dr])
        def _(dr=dr):
            rows_copy(dr).wait_send()
            rows_copy(-dr).wait_recv()
    u1[:, 8:16, :] = side_rows[0]
    u1[:, 24:32, :] = side_rows[1]
    add_spread(u1, x1, spread, 32, 3, 24)
    sweep(a1, w1, x1, u1)
    sweep(a1, w1, u1, x1)

    y = jnp.concatenate([x1[k, 8:32] for k in range(3)], 0)
    parts = []
    for b in range(2):
        z = dot(y[:, 128 * b : 128 * b + 128], wide)
        parts += [z[:, :128], z[:, 128:]]
    parts.append(dot(y[:, 256:384], ring_spread(SIDE, SIDE, 64)))
    add_spread(u0, x0, spread_rows(parts, st), 48, 5, 32, row0=8)
    sweep(a0, w0, x0, u0)
    for q in range(1, 1 + h // 8):
        mid, res = residual_at(a0, w0, u0, q)
        for k in range(3):
            new = mid[k] + w0[3 + k, 8 * q : 8 * q + 8] * res[k]
            out[k, 8 * q - 8 : 8 * q, :] = new[:, own_cols]

    for dr, dc in ways:
        @when(rowhas[dr], has[dc])
        def _(dr=dr, dc=dc):
            halo(dr, dc).wait_send()
    for dt, dc in partners:
        @when(has[dc])
        def _(dt=dt, dc=dc):
            gather(*coef, dt, dc).wait_send()
            gather(*src, dt, dc).wait_send()


def on_device(right_side, noise_block, edges):
    T, NB, NS = lax.axis_size("tiles"), lax.axis_size("band"), lax.axis_size("stokes")
    _, h, w = right_side.shape
    shapes = [
        (h + 2 * HALO, w + SIDE),
        (h // 2 + 16, w // 2 + SIDE),
        (h // 4 * T, 2 * SIDE),
        (max(8, h // 8 * T), SIDE),
        (max(8, h // 16 * T), SIDE),
    ]
    scratch = []
    for i, (n, m) in enumerate(shapes):
        scratch += [
            pltpu.VMEM((11, n, m), F32),
            pltpu.VMEM((3, n + 16, m), F32),
            pltpu.VMEM((3, n + 16, m), F32),
            pltpu.VMEM((6, n, m), F32),
        ]
        if i < 4:
            scratch.append(pltpu.VMEM((3 * n, m), F32))
    scratch += [
        pltpu.VMEM((BUFFERS, 5, max(6 * 32, 6 * h // 4 * T), SIDE), F32),
        pltpu.VMEM((48, 2 * SIDE), F32),
        pltpu.VMEM((2, h, SIDE), F32),
        pltpu.VMEM((2, h + 2 * HALO, SIDE), F32),
        pltpu.VMEM((2, sum(NEAR_ROWS), w), F32),
        pltpu.VMEM((2, sum(NEAR_ROWS), w), F32),
        pltpu.VMEM((T, 32, SIDE), F32),
        pltpu.VMEM((T, 2, 16, SIDE), F32),
        pltpu.VMEM((2, 16, SIDE), F32),
        pltpu.VMEM((T, 16, SIDE), F32),
        pltpu.VMEM((T, 2, 8, SIDE), F32),
        pltpu.VMEM((2, 8, SIDE), F32),
        pltpu.VMEM((2, 3, 8, 3 * SIDE), F32),
        pltpu.SemaphoreType.DMA((1,)),
        pltpu.SemaphoreType.DMA((9,)),
        pltpu.SemaphoreType.DMA((9,)),
        pltpu.SemaphoreType.DMA((T, 3)),
        pltpu.SemaphoreType.DMA((T, 3)),
        pltpu.SemaphoreType.DMA((T, 3)),
        pltpu.SemaphoreType.DMA((T, 3)),
        pltpu.SemaphoreType.DMA((2,)),
        pltpu.SemaphoreType.DMA((2,)),
    ]
    return pl.pallas_call(
        functools.partial(kernel, T, NB, NS),
        out_shape=jax.ShapeDtypeStruct(right_side.shape, F32),
        in_specs=[pl.BlockSpec(memory_space=pltpu.VMEM)],
        out_specs=pl.BlockSpec(memory_space=pltpu.VMEM),
        scratch_shapes=scratch,
        compiler_params=pltpu.CompilerParams(
            collective_id=0, has_side_effects=True, vmem_limit_bytes=40 * 1024 * 1024
        ),
    )(jnp.concatenate([right_side, noise_block, edges], 0))


def solution(mesh):
    spec = P(None, ("groups", "tiles"), ("band", "stokes"))
    return jax.shard_map(
        on_device, mesh=mesh, in_specs=(spec, spec, spec), out_specs=spec, check_vma=False
    )
```

profile of v0, /device:TPU:1, one launch (start us, length us, event | category | flops | bytes accessed | tf_op | source)
XLA Modules:
  0.0 20.6 jit_solution(12876856156485123012)
XLA Ops:
  0.0 1.1 %pad_maximum_fusion.stack = f32[11,16,512]{2,1,0:T(8,128)S(1)} fusion(f32[2,16,512]{2,1,0:T(8,128)} %param.5, f32[6,16,512]{2,1,0:T(8,128)} %param.4, f32[3,16,512]{2,1,0:T(8,128)} %param.3), kind=kLoop, calls=%fused_computation | loop fusion | flops 180224 | bytes 720896 | tf_op jit(solution)/shard_map/concatenate | solution.py:581
  1.1 18.9 %shard_map.37 = f32[3,16,512]{2,1,0:T(8,128)S(1)} custom-call(f32[11,16,512]{2,1,0:T(8,128)S(1)} %pad_maximum_fusion.stack), custom_call_target="tpu_custom_call" | custom-call | tf_op jit(solution)/shard_map/pallas_call | solution.py:572
  20.0 0.6 %copy.5 = f32[3,16,512]{2,1,0:T(8,128)} copy(f32[3,16,512]{2,1,0:T(8,128)S(1)} %shard_map.37) | data formatting | bytes 196608
where the time goes:
time: 20.8 us; the launch traced here: 20.6 us
  Pallas kernels  18.9 us (91%)
  other arithmetic  1.05 us (5%)
  local copies, waits for them, and re-layouts  0.64 us (3%)
    pallas_call x1, Pallas kernels, on_device(): pl.pallas_call(functools.partial(kernel, T, NB, NS), out_shape=jax.ShapeD...  18.9 us
    concatenate x1, other arithmetic, on_device(): jnp.concatenate([right_side, noise_block, edges], 0)  1.05 us
    unnamed x1, local copies, waits for them, and re-layouts  0.64 us

commit v1 on v0

--- a/solution.py
+++ b/solution.py
@@ -26,11 +26,9 @@
 def dot(x, y):
     n = x.shape[0]
     high = rounded(x)
-    rest = x - high
-    mid = rounded(rest)
-    pieces = jnp.concatenate([high, mid, rest - mid], 0)
+    pieces = jnp.concatenate([high, x - high], 0)
     z = jnp.dot(pieces, y, precision=lax.Precision.DEFAULT, preferred_element_type=F32)
-    return z[:n] + (z[n : 2 * n] + z[2 * n :])
+    return z[:n] + z[n:]
 
 
 def iota(shape, dim):
@@ -466,21 +464,36 @@
         n = a.shape[1] // 2
         for k in range(3):
             put(b, k, 0, [z[k * n : k * n + n] for z in source])
-    first(a4, w4, x4)
-    now, then = x4, u4
-    for _ in range(COARSE_SWEEPS - 1):
-        sweep(a4, w4, now, then)
-        now, then = then, now
-    coarse = now
+    if h // 16 * T < 8:
+        n = [a4[3 + i] for i in range(6)]
+        down, right, up, left, total = a4[9], a4[10], w4[0], w4[1], w4[2]
+        source, scale = [a4[k] for k in range(3)], [w4[3 + k] for k in range(3)]
+        v = [scale[k] * source[k] for k in range(3)]
+        weight = [n[k] + total for k in range(3)]
+        for _ in range(COARSE_SWEEPS - 1):
+            cross = [n[3] * v[1] + n[4] * v[2], n[3] * v[0] + n[5] * v[2], n[4] * v[0] + n[5] * v[1]]
+            new = []
+            for k in range(3):
+                near = (down * pltpu.roll(v[k], 7, 0) + up * pltpu.roll(v[k], 1, 0)) + (
+                    right * pltpu.roll(v[k], SIDE - 1, 1) + left * pltpu.roll(v[k], 1, 1)
+                )
+                new.append(v[k] + scale[k] * (source[k] - (weight[k] * v[k] + cross[k]) + near))
+            v = new
+    else:
+        first(a4, w4, x4)
+        now, then = x4, u4
+        for _ in range(COARSE_SWEEPS - 1):
+            sweep(a4, w4, now, then)
+            now, then = then, now
+        v = [now[k, 8 : 8 + a4.shape[1]] for k in range(3)]
     for a, aux, x, u in ((a3, w3, x3, u3), (a2, w2, x2, u2)):
-        n = coarse.shape[1] - 16
-        y = jnp.concatenate([coarse[k, 8 : 8 + n] for k in range(3)], 0)
-        z = dot(y, wide if a is a2 else ring_spread(SIDE, SIDE, 96))
+        n = v[0].shape[0]
+        z = dot(jnp.concatenate(v, 0), wide if a is a2 else ring_spread(SIDE, SIDE, 96))
         parts = [z[:, b : b + SIDE] for b in range(0, z.shape[1], SIDE)]
         add_spread(u, x, spread_rows(parts, st), 2 * n, len(parts), a.shape[1])
         sweep(a, aux, x, u)
         sweep(a, aux, u, x)
-        coarse = x
+        v = [x[k, 8 : 8 + a.shape[1]] for k in range(3)]
 
     for s in range(T):
         @pl.when(t == s)

time: 20.8 us -> 20.6 us (level)
  no operation moved by 1% of the time
where the time goes in v1:
time: 20.6 us; the launch traced here: 20.4 us
  Pallas kernels  18.7 us (91%)
  other arithmetic  1.05 us (5%)
  local copies, waits for them, and re-layouts  0.64 us (3%)
    pallas_call x1, Pallas kernels, on_device(): pl.pallas_call(functools.partial(kernel, T, NB, NS), out_shape=jax.ShapeD...  18.7 us
    concatenate x1, other arithmetic, on_device(): jnp.concatenate([right_side, noise_block, edges], 0)  1.05 us
    unnamed x1, local copies, waits for them, and re-layouts  0.64 us

profile of v1, /device:TPU:1, one launch (start us, length us, event | category | flops | bytes accessed | tf_op | source)
XLA Modules:
  0.0 20.4 jit_solution(4187107572828970096)
XLA Ops:
  0.0 1.1 %pad_maximum_fusion.stack = f32[11,16,512]{2,1,0:T(8,128)S(1)} fusion(f32[2,16,512]{2,1,0:T(8,128)} %param.5, f32[6,16,512]{2,1,0:T(8,128)} %param.4, f32[3,16,512]{2,1,0:T(8,128)} %param.3), kind=kLoop, calls=%fused_computation | loop fusion | flops 180224 | bytes 720896 | tf_op jit(solution)/shard_map/concatenate | solution.py:594
  1.1 18.7 %shard_map.37 = f32[3,16,512]{2,1,0:T(8,128)S(1)} custom-call(f32[11,16,512]{2,1,0:T(8,128)S(1)} %pad_maximum_fusion.stack), custom_call_target="tpu_custom_call" | custom-call | tf_op jit(solution)/shard_map/pallas_call | solution.py:585
  19.8 0.6 %copy.5 = f32[3,16,512]{2,1,0:T(8,128)} copy(f32[3,16,512]{2,1,0:T(8,128)S(1)} %shard_map.37) | data formatting | bytes 196608

commit v2 on v1

--- a/solution.py
+++ b/solution.py
@@ -226,53 +226,21 @@
         def _(dt=dt, dc=dc):
             pl.semaphore_signal(barrier, inc=1, device_id=device(lax.rem(t + dt, T), dc), device_id_type=MESH)
 
-    @pl.when(t == 0)
-    def _():
-        got[:, 0:HALO] = jnp.zeros_like(got[:, 0:HALO])
-        side_rows[0] = jnp.zeros_like(side_rows[0])
-
-    @pl.when(t == T - 1)
-    def _():
-        got[:, HALO + h :] = jnp.zeros_like(got[:, HALO + h :])
-        side_rows[1] = jnp.zeros_like(side_rows[1])
-
-    @pl.when(col == 0)
-    def _():
-        got[0] = jnp.zeros_like(got[0])
-        coef_side[:, 0] = jnp.zeros_like(coef_side[:, 0])
-        src_side[:, 0] = jnp.zeros_like(src_side[:, 0])
-
-    @pl.when(col == cols - 1)
-    def _():
-        got[1] = jnp.zeros_like(got[1])
-        coef_side[:, 1] = jnp.zeros_like(coef_side[:, 1])
-        src_side[:, 1] = jnp.zeros_like(src_side[:, 1])
-
-    a0[:, 0:HALO, own_cols] = jnp.zeros_like(a0[:, 0:HALO, own_cols])
-    a0[:, HALO + h :, own_cols] = jnp.zeros_like(a0[:, HALO + h :, own_cols])
-    for a in (a1, a3, a4):
-        a[...] = jnp.zeros_like(a)
-    for v in (x0, u0, x1, u1, x2, u2, x3, u3, x4, u4):
-        v[:, 0:8, :] = jnp.zeros_like(v[:, 0:8, :])
-        n = v.shape[1]
-        v[:, n - 8 : n, :] = jnp.zeros_like(v[:, n - 8 : n, :])
-
-    load.wait()
 
     lane = iota((8, SIDE), 1)
     for q in range(h // 8):
-        rows = slice(HALO + 8 * q, HALO + 8 * q + 8)
+        rows = slice(8 * q, 8 * q + 8)
         head = tail = jnp.zeros((8, SIDE), F32)
         for i in range(11):
             here = (lane >= DEEP * i) & (lane < DEEP * i + DEEP)
-            one, two = a0[i, rows, 0:SIDE], a0[i, rows, w - SIDE : w]
+            one, two = stack[i, rows, 0:SIDE], stack[i, rows, w - SIDE : w]
             head = jnp.where(here, pltpu.roll(one, DEEP * i, 1) if i else one, head)
             tail = jnp.where(here, pltpu.roll(two, (DEEP * i + DEEP) % SIDE, 1), tail)
         sent[0, 8 * q : 8 * q + 8], sent[1, 8 * q : 8 * q + 8] = head, tail
     at = 0
     for i, n in enumerate(NEAR_ROWS):
-        rows_sent[0, at : at + n] = a0[i, HALO : HALO + n, own_cols]
-        rows_sent[1, at : at + n] = a0[i, HALO + h - n : HALO + h, own_cols]
+        rows_sent[0, at : at + n] = stack[i, 0:n]
+        rows_sent[1, at : at + n] = stack[i, h - n : h]
         at += n
 
     sides = 1 + jnp.where(col > 0, 1, 0) + jnp.where(col < cols - 1, 1, 0)
@@ -303,6 +271,37 @@
         def _(dr=dr, dc=dc):
             halo(dr, dc).start()
 
+    @pl.when(t == 0)
+    def _():
+        got[:, 0:HALO] = jnp.zeros_like(got[:, 0:HALO])
+        side_rows[0] = jnp.zeros_like(side_rows[0])
+
+    @pl.when(t == T - 1)
+    def _():
+        got[:, HALO + h :] = jnp.zeros_like(got[:, HALO + h :])
+        side_rows[1] = jnp.zeros_like(side_rows[1])
+
+    @pl.when(col == 0)
+    def _():
+        got[0] = jnp.zeros_like(got[0])
+        coef_side[:, 0] = jnp.zeros_like(coef_side[:, 0])
+        src_side[:, 0] = jnp.zeros_like(src_side[:, 0])
+
+    @pl.when(col == cols - 1)
+    def _():
+        got[1] = jnp.zeros_like(got[1])
+        coef_side[:, 1] = jnp.zeros_like(coef_side[:, 1])
+        src_side[:, 1] = jnp.zeros_like(src_side[:, 1])
+
+    a0[:, 0:HALO, own_cols] = jnp.zeros_like(a0[:, 0:HALO, own_cols])
+    a0[:, HALO + h :, own_cols] = jnp.zeros_like(a0[:, HALO + h :, own_cols])
+    for a in (a1, a3, a4):
+        a[...] = jnp.zeros_like(a)
+    for v in (x0, u0, x1, u1, x2, u2, x3, u3, x4, u4):
+        v[:, 0:8, :] = jnp.zeros_like(v[:, 0:8, :])
+        n = v.shape[1]
+        v[:, n - 8 : n, :] = jnp.zeros_like(v[:, n - 8 : n, :])
+
     def gather(own, side, pack, send, recv, dt, dc):
         if dc:
             src, dst = pack.at[(dc + 1) // 2], side.at[t, (1 - dc) // 2]
@@ -371,7 +370,7 @@
     even_ring, odd_ring = ring_pool(64), ring_pool(64, odd=True)
     wide = spread_matrix(128, 256)
 
-    fine = [a0[3 + i, own_rows, own_cols] for i in range(8)]
+    fine = [stack[3 + i] for i in range(8)]
     mid = coarsen_coefficients(fine, st, even, odd)
     for i in range(8):
         put(a1, 3 + i, 8, mid[i])
@@ -407,6 +406,8 @@
                 top = HALO - n if dr < 0 else HALO + h
                 a0[i, top : top + n, own_cols] = rows_got[(dr + 1) // 2, at : at + n]
                 at += n
+
+    load.wait()
 
     setup(a0, w0)
     first(a0, w0, x0)

time: 20.6 us -> 20.5 us (level)
  no operation moved by 1% of the time
where the time goes in v2:
time: 20.5 us; the launch traced here: 20.4 us
  Pallas kernels  18.7 us (91%)
  other arithmetic  1.05 us (5%)
  local copies, waits for them, and re-layouts  0.64 us (3%)
    pallas_call x1, Pallas kernels, on_device(): pl.pallas_call(functools.partial(kernel, T, NB, NS), out_shape=jax.ShapeD...  18.7 us
    concatenate x1, other arithmetic, on_device(): jnp.concatenate([right_side, noise_block, edges], 0)  1.05 us
    unnamed x1, local copies, waits for them, and re-layouts  0.64 us

profile of v2, /device:TPU:1, one launch (start us, length us, event | category | flops | bytes accessed | tf_op | source)
XLA Modules:
  0.0 20.4 jit_solution(4463216035480053243)
XLA Ops:
  0.0 1.1 %pad_maximum_fusion.stack = f32[11,16,512]{2,1,0:T(8,128)S(1)} fusion(f32[2,16,512]{2,1,0:T(8,128)} %param.5, f32[6,16,512]{2,1,0:T(8,128)} %param.4, f32[3,16,512]{2,1,0:T(8,128)} %param.3), kind=kLoop, calls=%fused_computation | loop fusion | flops 180224 | bytes 720896 | tf_op jit(solution)/shard_map/concatenate | solution.py:595
  1.1 18.7 %shard_map.37 = f32[3,16,512]{2,1,0:T(8,128)S(1)} custom-call(f32[11,16,512]{2,1,0:T(8,128)S(1)} %pad_maximum_fusion.stack), custom_call_target="tpu_custom_call" | custom-call | tf_op jit(solution)/shard_map/pallas_call | solution.py:586
  19.7 0.6 %copy.5 = f32[3,16,512]{2,1,0:T(8,128)} copy(f32[3,16,512]{2,1,0:T(8,128)S(1)} %shard_map.37) | data formatting | bytes 196608

commit v3 on v2

--- a/solution.py
+++ b/solution.py
@@ -409,6 +409,14 @@
 
     load.wait()
 
+    beside = [
+        jnp.concatenate([a0[3 + i, 0:HALO, own_cols], a0[3 + i, HALO + h :, own_cols]], 0) for i in range(8)
+    ]
+    for i, parts in enumerate(coarsen_coefficients(beside, st, even, odd)):
+        put(a1, 3 + i, 4, [p[:4] for p in parts])
+        put(a1, 3 + i, 16, [p[4:] for p in parts])
+    setup(a1, w1)
+
     setup(a0, w0)
     first(a0, w0, x0)
     sweep(a0, w0, x0, u0)
@@ -417,13 +425,6 @@
     h1 = a0.shape[1] // 2
     for k in range(3):
         put(a1, k, 4, [p[k * h1 : k * h1 + h1] for p in source])
-    beside = [
-        jnp.concatenate([a0[3 + i, 0:HALO, own_cols], a0[3 + i, HALO + h :, own_cols]], 0) for i in range(8)
-    ]
-    for i, parts in enumerate(coarsen_coefficients(beside, st, even, odd)):
-        put(a1, 3 + i, 4, [p[:4] for p in parts])
-        put(a1, 3 + i, 16, [p[4:] for p in parts])
-    setup(a1, w1)
     first(a1, w1, x1)
     sweep(a1, w1, x1, u1)
     residual(a1, w1, u1, r1)

time: 20.5 us -> 20.5 us (level)
  no operation moved by 1% of the time
where the time goes in v3:
time: 20.5 us; the launch traced here: 20.3 us
  Pallas kernels  18.6 us (91%)
  other arithmetic  1.05 us (5%)
  local copies, waits for them, and re-layouts  0.64 us (3%)
    pallas_call x1, Pallas kernels, on_device(): pl.pallas_call(functools.partial(kernel, T, NB, NS), out_shape=jax.ShapeD...  18.6 us
    concatenate x1, other arithmetic, on_device(): jnp.concatenate([right_side, noise_block, edges], 0)  1.05 us
    unnamed x1, local copies, waits for them, and re-layouts  0.64 us

profile of v3, /device:TPU:1, one launch (start us, length us, event | category | flops | bytes accessed | tf_op | source)
XLA Modules:
  0.0 20.3 jit_solution(17929655544871867318)
XLA Ops:
  0.0 1.1 %pad_maximum_fusion.stack = f32[11,16,512]{2,1,0:T(8,128)S(1)} fusion(f32[2,16,512]{2,1,0:T(8,128)} %param.5, f32[6,16,512]{2,1,0:T(8,128)} %param.4, f32[3,16,512]{2,1,0:T(8,128)} %param.3), kind=kLoop, calls=%fused_computation | loop fusion | flops 180224 | bytes 720896 | tf_op jit(solution)/shard_map/concatenate | solution.py:596
  1.1 18.6 %shard_map.37 = f32[3,16,512]{2,1,0:T(8,128)S(1)} custom-call(f32[11,16,512]{2,1,0:T(8,128)S(1)} %pad_maximum_fusion.stack), custom_call_target="tpu_custom_call" | custom-call | tf_op jit(solution)/shard_map/pallas_call | solution.py:587
  19.7 0.6 %copy.5 = f32[3,16,512]{2,1,0:T(8,128)} copy(f32[3,16,512]{2,1,0:T(8,128)S(1)} %shard_map.37) | data formatting | bytes 196608
